TPU v7x, 32 devices: a whole 2x2x4 slice. The times are simulated.
32 devices in a mesh: ckpt: 4 (over y, x), vocab: 8 (over z, core).
Axes of the slice: x: 2, y: 2, z: 4, core: 2. Of those that a mesh axis runs over, the one named last changes fastest.
Arguments:
- token_ids: int32 [1024], P('vocab'), may hold values from 0 to 1023, as said below
- grad_values: bfloat16 [4, 1024, 8192], P('ckpt', 'vocab'), may hold values from -6 to 6
- grad_scales: float32 [4, 64, 1024], P('ckpt', None, 'vocab'), may hold values from 0.3 to 3
- tables: bfloat16 [4, 1024, 8192], P('ckpt', 'vocab'), may hold values from -6 to 6
Outputs:
- merged: bfloat16 [1024, 8192], P('vocab', 'ckpt')
Inputs may be any that keep to these rules, and one draw needn't show every extreme that they name: The owner of a token is token_ids // 128. Among the 128 tokens of each index of vocab, exactly 4 owners appear, each with exactly 32 tokens; one owner appears in every index's tokens. Ids repeat and some owners are far more frequent than others.
All inputs are finite; a program needn't handle non-finite values.
Results may differ from a plain program's by a relative error of at most 0.018.
Values may be sent and summed in bfloat16 or wider, within the bound.
A program may use at most 64 MiB of HBM per device.

v0:
```python
import jax
import jax.numpy as jnp
from jax import lax
from jax.sharding import PartitionSpec as P

BLK = 128


prior_weight = 1.0


def per_device(token_ids, grad_values, grad_scales, tables):
    groups = lax.axis_size("vocab")
    rows = tables.shape[1]
    width = tables.shape[2]
    count = token_ids.shape[0]
    capacity = 2 * count // groups
    owner = token_ids // rows
    same = owner[:, None] == owner[None, :]
    before = lax.broadcasted_iota(jnp.int32, (count, count), 0) < lax.broadcasted_iota(
        jnp.int32, (count, count), 1
    )
    rank = jnp.sum((same & before).astype(jnp.int32), axis=0)
    slot = owner * capacity + rank
    match = lax.broadcasted_iota(jnp.int32, (groups * capacity, count), 0) == slot[None, :]
    scales = grad_scales[0].T
    grads = (
        grad_values[0].astype(jnp.float32).reshape(count, width // BLK, BLK) * scales[:, :, None]
    )
    squares = (grads * grads).reshape(count, width).astype(jnp.bfloat16)
    placed = jnp.dot(match.astype(jnp.bfloat16), squares, preferred_element_type=jnp.float32)
    buffer = placed.astype(jnp.bfloat16).reshape(groups, capacity, width)
    local_rows = token_ids % rows
    row_tags = (
        jnp.sum(jnp.where(match, local_rows[None, :], 0), axis=1)
        .astype(jnp.bfloat16)
        .reshape(groups, capacity)
    )
    arrived, arrived_rows = (
        lax.all_to_all(buffer, "vocab", split_axis=0, concat_axis=0, tiled=True),
        lax.all_to_all(row_tags, "vocab", split_axis=0, concat_axis=0, tiled=True),
    )
    flat_rows = arrived_rows.reshape(groups * capacity).astype(jnp.int32)
    selector = (
        lax.broadcasted_iota(jnp.int32, (rows, groups * capacity), 0) == flat_rows[None, :]
    ).astype(jnp.bfloat16)
    fisher = jnp.dot(
        selector, arrived.reshape(groups * capacity, width), preferred_element_type=jnp.float32
    )
    weight = (fisher + prior_weight).astype(jnp.bfloat16)
    term = (weight.astype(jnp.float32) * tables[0].astype(jnp.float32)).astype(jnp.bfloat16)
    numer, denom = (
        lax.psum_scatter(term, "ckpt", scatter_dimension=1, tiled=True).astype(jnp.float32),
        lax.psum_scatter(weight, "ckpt", scatter_dimension=1, tiled=True).astype(jnp.float32),
    )
    return (numer / denom).astype(jnp.bfloat16)


def solution(mesh):
    return jax.shard_map(
        per_device,
        mesh=mesh,
        in_specs=(
            P("vocab"),
            P("ckpt", "vocab", None),
            P("ckpt", None, "vocab"),
            P("ckpt", "vocab", None),
        ),
        out_specs=P("vocab", "ckpt"),
        check_vma=False,
    )
```

profile of v0, /device:TPU:0, one launch (start us, length us, event | category | flops | bytes accessed | tf_op | source)
XLA Modules:
  0.0 207.9 jit_solution(8382496772177393412)
XLA Ops:
  6.5 0.0 copy-start
  6.5 0.8 and_select_fusion
  7.4 0.1 convert_reduce_fusion
  7.5 0.1 select_reduce_fusion
  7.6 0.7 convert_element_type.87
  8.3 6.3 %all-to-all-start = ((bf16[8,1,32]{2,1,0:T(2,128)(2,1)}), bf16[8,1,32]{2,1,0:T(2,128)(2,1)S(1)}, u32[]{:S(2)}, u32[]{:S(2)}) async-start(bf16[8,1,32]{2,1,0:T(2,128)(2,1)} %convert_element_type.87), calls=%async_computation | async-start | bytes 8192 | tf_op jit(solution)/shard_map/all_to_all | solution.py:41
  14.6 0.8 copy.10
  15.4 1.1 mul.26
  16.6 0.0 copy-done
  16.6 5.1 %convolution_convert_fusion = bf16[256,8192]{1,0:T(8,128)(2,1)} fusion(f32[16,8,64,128]{3,2,1,0:T(8,128)S(1)} %bitcast.24, bf16[1,128,8192]{2,1,0:T(8,128)(2,1)S(1)} %copy-done, s32[128]{0:T(128)S(1)} %multiply_add_fusion), kind=kOutput, calls=%fused_computation | convolution fusion | flops 543195136 | bytes 10486272 | tf_op jit(solution)/shard_map/dot_general | solution.py:31
  21.7 0.0 all-to-all-done
  21.7 0.0 copy-start.1
  21.7 5.2 %all-to-all-start.1 = ((bf16[8,32,8192]{2,1,0:T(8,128)(2,1)}), bf16[8,32,8192]{2,1,0:T(8,128)(2,1)}, u32[]{:S(2)}, u32[]{:S(2)}) async-start(bf16[8,32,8192]{2,1,0:T(8,128)(2,1)} %bitcast.23), calls=%async_computation.1 | async-start | bytes 8388608 | tf_op jit(solution)/shard_map/all_to_all | solution.py:40
  26.9 0.0 reduce-scatter.3.cloned.1.call-start
  27.0 0.1 reshape.46
  27.1 94.0 %all-to-all-done.1 = bf16[8,32,8192]{2,1,0:T(8,128)(2,1)} async-done(((bf16[8,32,8192]{2,1,0:T(8,128)(2,1)}), bf16[8,32,8192]{2,1,0:T(8,128)(2,1)}, u32[]{:S(2)}, u32[]{:S(2)}) %all-to-all-start.1) | async-done | bytes 4194336 | tf_op jit(solution)/shard_map/all_to_all | solution.py:40
  121.1 0.0 copy-done.1
  121.1 5.1 %fusion.3 = (bf16[128,8192]{1,0:T(8,128)(2,1)}, bf16[128,8192]{1,0:T(8,128)(2,1)}) fusion(bf16[1,128,8192]{2,1,0:T(8,128)(2,1)S(1)} %copy-done.1, bf16[256,8192]{1,0:T(8,128)(2,1)} %bitcast.4, s32[256]{0:T(256)S(1)} %reshape.46), kind=kOutput, calls=%fused_computation.7 | convolution fusion | flops 543195136 | bytes 10486784 | tf_op jit(solution)/shard_map/dot_general | solution.py:47
  126.2 0.0 reduce-scatter.3.cloned.1.call-update
  126.2 0.0 reduce-scatter.5.cloned.1.call-start
  126.2 0.7 reduce-scatter.5.cloned.1.call-update
  126.9 33.5 %reduce-scatter.3.cloned.1.call-done = bf16[128,2048]{1,0:T(8,128)(2,1)} async-done(((bf16[128,8192]{1,0:T(8,128)(2,1)}), bf16[128,2048]{1,0:T(8,128)(2,1)}) %reduce-scatter.3.cloned.1.call-update) | async-done | bytes 524304 | tf_op jit(solution)/shard_map/reduce_scatter | solution.py:53
  160.4 38.4 %reduce-scatter.5.cloned.1.call-done = bf16[128,2048]{1,0:T(8,128)(2,1)} async-done(((bf16[128,8192]{1,0:T(8,128)(2,1)}), bf16[128,2048]{1,0:T(8,128)(2,1)}) %reduce-scatter.5.cloned.1.call-update) | async-done | bytes 524304 | tf_op jit(solution)/shard_map/reduce_scatter | solution.py:54
  198.9 2.2 %divide_convert_fusion = bf16[128,2048]{1,0:T(8,128)(2,1)} fusion(bf16[128,2048]{1,0:T(8,128)(2,1)} %reduce-scatter.5.cloned.1.call-done, bf16[128,2048]{1,0:T(8,128)(2,1)} %reduce-scatter.3.cloned.1.call-done), kind=kLoop, calls=%fused_computation.9 | loop fusion | flops 1048576 | bytes 1572864 | tf_op jit(solution)/shard_map/convert_element_type | solution.py:56
  (3 shorter events, 0.0 us)
Async XLA Ops:
  6.5 10.1 %copy-start = (bf16[1,128,8192]{2,1,0:T(8,128)(2,1)S(1)}, bf16[1,128,8192]{2,1,0:T(8,128)(2,1)}, u32[]{:S(2)}) copy-start(bf16[1,128,8192]{2,1,0:T(8,128)(2,1)} %param.5) | copy-start | bytes 6291460
  8.3 13.4 %all-to-all-start = ((bf16[8,1,32]{2,1,0:T(2,128)(2,1)}), bf16[8,1,32]{2,1,0:T(2,128)(2,1)S(1)}, u32[]{:S(2)}, u32[]{:S(2)}) async-start(bf16[8,1,32]{2,1,0:T(2,128)(2,1)} %convert_element_type.87), calls=%async_computation | async-start | bytes 8192 | tf_op jit(solution)/shard_map/all_to_all | solution.py:41
  21.7 99.4 %copy-start.1 = (bf16[1,128,8192]{2,1,0:T(8,128)(2,1)S(1)}, bf16[1,128,8192]{2,1,0:T(8,128)(2,1)}, u32[]{:S(2)}) copy-start(bf16[1,128,8192]{2,1,0:T(8,128)(2,1)} %param.7) | copy-start | bytes 6291460
  21.7 99.3 %all-to-all-start.1 = ((bf16[8,32,8192]{2,1,0:T(8,128)(2,1)}), bf16[8,32,8192]{2,1,0:T(8,128)(2,1)}, u32[]{:S(2)}, u32[]{:S(2)}) async-start(bf16[8,32,8192]{2,1,0:T(8,128)(2,1)} %bitcast.23), calls=%async_computation.1 | async-start | bytes 8388608 | tf_op jit(solution)/shard_map/all_to_all | solution.py:40
  26.9 133.5 %reduce-scatter.3.cloned.1.call-start = ((), (), s32[]{:S(2)}) async-start(), calls=%async_computation.4 | async-start | bytes 2621440 | tf_op jit(solution)/shard_map/reduce_scatter | solution.py:53
  126.2 72.7 %reduce-scatter.5.cloned.1.call-start = ((), (), s32[]{:S(2)}) async-start(), calls=%async_computation.5 | async-start | bytes 2621440 | tf_op jit(solution)/shard_map/reduce_scatter | solution.py:54
Sparse Core Ops, SparseCore 0:
  126.3 34.0 reduce-scatter.2
  163.7 35.1 reduce-scatter.4
where the time goes:
time: 208 us
  waiting for transfers between devices  167 us (80%)
  between operations  13.4 us (6%)
  starting transfers between devices  11.6 us (6%)
  matrix products  10.2 us (5%)
  other arithmetic  3.22 us (2%)
  local copies, waits for them, and re-layouts  2.76 us (1%)
    all_to_all x1, waiting for transfers between devices, per_device(): lax.all_to_all(buffer, 'vocab', split_axis=0, concat_axis=0, tiled=True)  94 us
    reduce_scatter x1, waiting for transfers between devices, per_device(): lax.psum_scatter(weight, 'ckpt', scatter_dimension=1, tiled=True)  38.4 us
    reduce_scatter x1, waiting for transfers between devices, per_device(): lax.psum_scatter(term, 'ckpt', scatter_dimension=1, tiled=True)  33.5 us
    all_to_all x1, starting transfers between devices, per_device(): lax.all_to_all(row_tags, 'vocab', split_axis=0, concat_axis=0, tiled=True)  6.33 us
    all_to_all x1, starting transfers between devices, per_device(): lax.all_to_all(buffer, 'vocab', split_axis=0, concat_axis=0, tiled=True)  5.23 us
    dot_general x1, matrix products, per_device(): jnp.dot(selector, arrived.reshape(groups * capacity, width), preferred_el...  5.11 us
    dot_general x1, matrix products, per_device(): jnp.dot(match.astype(jnp.bfloat16), squares, preferred_element_type=jnp.f...  5.09 us
  transfers between devices with their start and end apart: 4, of which 3 were waited for; matrix products, arithmetic and copies ran while one was open for 3% of the time, Pallas kernels for 0%

commit v1 on v0

--- a/solution.py
+++ b/solution.py
@@ -1,15 +1,281 @@
+import functools
+
 import jax
 import jax.numpy as jnp
 from jax import lax
+from jax.experimental import pallas as pl
+from jax.experimental.pallas import tpu as pltpu
 from jax.sharding import PartitionSpec as P
 
 BLK = 128
+CHUNKS = 8
+MESH = pl.DeviceIdType.MESH
 
 
 prior_weight = 1.0
 
 
-def per_device(token_ids, grad_values, grad_scales, tables):
+def merge_kernel(
+    groups,
+    ckpts,
+    chunks,
+    ids_row_ref,
+    ids_col_ref,
+    grads_ref,
+    scales_ref,
+    tables_ref,
+    out_ref,
+    grads,
+    tables,
+    match_ref,
+    select_ref,
+    tag_send,
+    tag_recv,
+    send,
+    recv,
+    part_send,
+    part_recv,
+    load_sem,
+    tag_send_sem,
+    tag_recv_sem,
+    send_sem,
+    recv_sem,
+    part_send_sem,
+    part_recv_sem,
+):
+    c = lax.axis_index("ckpt")
+    v = lax.axis_index("vocab")
+    rows = tables.shape[0]
+    count = grads.shape[0]
+    width = grads.shape[1]
+    slots = match_ref.shape[0]
+    capacity = slots // groups
+    quarter = width // ckpts
+    piece = quarter // chunks
+    blocks = piece // BLK
+
+    def vocab_peer(j):
+        return (c, lax.rem(v + j, groups))
+
+    def ckpt_peer(j):
+        return (lax.rem(c + j, ckpts), v)
+
+    barrier = pltpu.get_barrier_semaphore()
+    for j in range(1, groups):
+        pl.semaphore_signal(barrier, inc=1, device_id=vocab_peer(j), device_id_type=MESH)
+    for j in range(1, ckpts):
+        pl.semaphore_signal(barrier, inc=1, device_id=ckpt_peer(j), device_id_type=MESH)
+
+    load_grads = pltpu.make_async_copy(grads_ref, grads, load_sem.at[0])
+    load_tables = pltpu.make_async_copy(tables_ref, tables, load_sem.at[1])
+    load_grads.start()
+    load_tables.start()
+
+    ids_row = ids_row_ref[...]
+    ids_col = ids_col_ref[...]
+    near_row = lax.rem(ids_row // rows - v + groups, groups)
+    near_col = lax.rem(ids_col // rows - v + groups, groups)
+    same = near_row == near_col
+    at0 = lax.broadcasted_iota(jnp.int32, (count, count), 0)
+    at1 = lax.broadcasted_iota(jnp.int32, (count, count), 1)
+    rank_row = jnp.sum(jnp.where(same & (at0 < at1), 1, 0), axis=0, keepdims=True)
+    rank_col = jnp.sum(jnp.where(same & (at1 < at0), 1, 0), axis=1, keepdims=True)
+    slot_row = near_row * capacity + rank_row
+    slot_col = near_col * capacity + rank_col
+    match_ref[...] = jnp.where(
+        lax.broadcasted_iota(jnp.int32, (slots, count), 0) == slot_row, 1.0, 0.0
+    ).astype(jnp.bfloat16)
+    tags = jnp.sum(
+        jnp.where(
+            lax.broadcasted_iota(jnp.int32, (count, slots), 1) == slot_col,
+            lax.rem(ids_col, rows),
+            0,
+        ),
+        axis=0,
+        keepdims=True,
+    )
+    tag_send[...] = jnp.broadcast_to(tags, tag_send.shape)
+
+    def tag_copy(j):
+        return pltpu.make_async_remote_copy(
+            src_ref=tag_send,
+            dst_ref=tag_recv.at[j],
+            send_sem=tag_send_sem.at[j],
+            recv_sem=tag_recv_sem.at[j],
+            device_id=vocab_peer(j),
+            device_id_type=MESH,
+        )
+
+    def row_copy(k, j):
+        return pltpu.make_async_remote_copy(
+            src_ref=send.at[k, j],
+            dst_ref=recv.at[k, j],
+            send_sem=send_sem.at[k, j],
+            recv_sem=recv_sem.at[k, j],
+            device_id=vocab_peer(j),
+            device_id_type=MESH,
+        )
+
+    def part_copy(k, j):
+        return pltpu.make_async_remote_copy(
+            src_ref=part_send.at[k, j],
+            dst_ref=part_recv.at[k, j],
+            send_sem=part_send_sem.at[k, j],
+            recv_sem=part_recv_sem.at[k, j],
+            device_id=ckpt_peer(j),
+            device_id_type=MESH,
+        )
+
+    order = sorted(range(1, groups), key=lambda j: -min(j, groups - j))
+
+    load_grads.wait()
+    pl.semaphore_wait(barrier, groups + ckpts - 2)
+    for j in order:
+        tag_copy(j).start()
+
+    def place(k, carry):
+        block_scales = jnp.concatenate(
+            [
+                scales_ref[pl.ds(q * (quarter // BLK) + k * blocks, blocks), :]
+                for q in range(ckpts)
+            ],
+            axis=0,
+        ).T
+        squares = []
+        for q in range(ckpts):
+            for b in range(blocks):
+                at = pl.multiple_of(q * quarter + k * piece + b * BLK, BLK)
+                i = q * blocks + b
+                g = grads[:, pl.ds(at, BLK)].astype(jnp.float32) * block_scales[:, i : i + 1]
+                squares.append((g * g).astype(jnp.bfloat16))
+        placed = jnp.dot(
+            match_ref[...],
+            jnp.concatenate(squares, axis=1),
+            preferred_element_type=jnp.float32,
+        ).astype(jnp.bfloat16)
+        placed = placed.reshape(groups, capacity, ckpts * piece)
+        recv[k, 0] = placed[0]
+        for j in range(1, groups):
+            send[k, j] = placed[j]
+        for j in order:
+            row_copy(k, j).start()
+        return carry
+
+    lax.fori_loop(0, chunks, place, 0)
+
+    lane = lax.broadcasted_iota(jnp.int32, (1, slots), 1) // capacity
+    arrived_tags = jnp.where(lane == 0, tags, 0)
+    for j in range(1, groups):
+        tag_copy(j).wait()
+        arrived_tags = jnp.where(lane == j, tag_recv[j, 0:1, :], arrived_tags)
+    select_ref[...] = jnp.where(
+        lax.broadcasted_iota(jnp.int32, (rows, slots), 0) == arrived_tags, 1.0, 0.0
+    ).astype(jnp.bfloat16)
+    load_tables.wait()
+
+    def weigh_chunk(k):
+        for j in range(1, groups):
+            row_copy(k, j).wait_recv()
+        fisher = jnp.dot(
+            select_ref[...],
+            recv[k].reshape(slots, ckpts * piece),
+            preferred_element_type=jnp.float32,
+        )
+        weight = (fisher + prior_weight).astype(jnp.bfloat16)
+        for q in range(ckpts):
+            own = weight[:, q * piece : (q + 1) * piece]
+            at = pl.multiple_of(q * quarter + k * piece, BLK)
+            table = tables[:, pl.ds(at, piece)].astype(jnp.float32)
+            j = lax.rem(q - c + ckpts, ckpts)
+            part_send[k, j, 0] = (own.astype(jnp.float32) * table).astype(jnp.bfloat16)
+            part_send[k, j, 1] = own
+        for j in range(1, ckpts):
+            part_copy(k, j).start()
+
+    def finish_chunk(k):
+        numer = part_send[k, 0, 0].astype(jnp.float32)
+        denom = part_send[k, 0, 1].astype(jnp.float32)
+        for j in range(1, ckpts):
+            part_copy(k, j).wait_recv()
+            numer += part_recv[k, j, 0].astype(jnp.float32)
+            denom += part_recv[k, j, 1].astype(jnp.float32)
+        at = pl.multiple_of(k * piece, BLK)
+        out_ref[:, pl.ds(at, piece)] = (numer / denom).astype(jnp.bfloat16)
+
+    weigh_chunk(0)
+
+    def step(k, carry):
+        weigh_chunk(k)
+        finish_chunk(k - 1)
+        return carry
+
+    lax.fori_loop(1, chunks, step, 0)
+    finish_chunk(chunks - 1)
+
+    def drain(k, carry):
+        for j in range(1, groups):
+            row_copy(k, j).wait_send()
+        for j in range(1, ckpts):
+            part_copy(k, j).wait_send()
+        return carry
+
+    lax.fori_loop(0, chunks, drain, 0)
+
+
+def merge_rows(token_ids, grad_values, grad_scales, tables):
+    groups = lax.axis_size("vocab")
+    ckpts = lax.axis_size("ckpt")
+    rows, width = tables.shape[1:]
+    count = token_ids.shape[0]
+    slots = 2 * count
+    capacity = slots // groups
+    chunk_width = width // CHUNKS
+    vmem = pl.BlockSpec(memory_space=pltpu.VMEM)
+    hbm = pl.BlockSpec(memory_space=pl.ANY)
+    bf16 = jnp.bfloat16
+    dma = pltpu.SemaphoreType.DMA
+    return pl.pallas_call(
+        functools.partial(merge_kernel, groups, ckpts, CHUNKS),
+        out_shape=jax.ShapeDtypeStruct((rows, width // ckpts), bf16),
+        in_specs=[vmem, vmem, hbm, vmem, hbm],
+        out_specs=vmem,
+        scratch_shapes=[
+            pltpu.VMEM((count, width), bf16),
+            pltpu.VMEM((rows, width), bf16),
+            pltpu.VMEM((slots, count), bf16),
+            pltpu.VMEM((rows, slots), bf16),
+            pltpu.VMEM((8, slots), jnp.int32),
+            pltpu.VMEM((groups, 8, slots), jnp.int32),
+            pltpu.VMEM((CHUNKS, groups, capacity, chunk_width), bf16),
+            pltpu.VMEM((CHUNKS, groups, capacity, chunk_width), bf16),
+            pltpu.VMEM((CHUNKS, ckpts, 2, rows, chunk_width // ckpts), bf16),
+            pltpu.VMEM((CHUNKS, ckpts, 2, rows, chunk_width // ckpts), bf16),
+            dma((2,)),
+            dma((groups,)),
+            dma((groups,)),
+            dma((CHUNKS, groups)),
+            dma((CHUNKS, groups)),
+            dma((CHUNKS, ckpts)),
+            dma((CHUNKS, ckpts)),
+        ],
+        compiler_params=pltpu.CompilerParams(
+            collective_id=0, has_side_effects=True, vmem_limit_bytes=48 * 1024 * 1024
+        ),
+        cost_estimate=pl.CostEstimate(
+            flops=4 * slots * count * width,
+            bytes_accessed=5 * rows * width,
+            transcendentals=0,
+        ),
+    )(
+        token_ids.reshape(1, count),
+        token_ids.reshape(count, 1),
+        grad_values[0],
+        grad_scales[0],
+        tables[0],
+    )
+
+
+def merge_small_slots(token_ids, grad_values, grad_scales, tables):
     groups = lax.axis_size("vocab")
     rows = tables.shape[1]
     width = tables.shape[2]
@@ -54,6 +320,17 @@
         lax.psum_scatter(weight, "ckpt", scatter_dimension=1, tiled=True).astype(jnp.float32),
     )
     return (numer / denom).astype(jnp.bfloat16)
+
+
+def per_device(token_ids, grad_values, grad_scales, tables):
+    groups = lax.axis_size("vocab")
+    ckpts = lax.axis_size("ckpt")
+    count = token_ids.shape[0]
+    width = tables.shape[2]
+    capacity = 2 * count // groups
+    if capacity % 16 == 0 and width % (ckpts * CHUNKS * BLK) == 0:
+        return merge_rows(token_ids, grad_values, grad_scales, tables)
+    return merge_small_slots(token_ids, grad_values, grad_scales, tables)
 
 
 def solution(mesh):

time: 208 us -> 112 us (0.54)
  waiting for transfers between devices: 167 us -> 0 us
  Pallas kernels: 0 us -> 106 us
  between operations: 13.4 us -> 0.02 us
  starting transfers between devices: 11.6 us -> 0 us
  matrix products: 10.2 us -> 0 us
  local copies, waits for them, and re-layouts: 2.76 us -> 6.15 us
  other arithmetic: 3.22 us -> 0 us
    pallas_call x0 -> x1, Pallas kernels: none -> 106 us  [merge_rows(): pl.pallas_call(functools.partial(merge_kernel, groups, ckpts, CHUNKS), ou...]
    all_to_all x2 -> x0, waiting for transfers between devices: 94 us -> none  [the longest x1 94 us: per_device(): lax.all_to_all(buffer, 'vocab', split_axis=0, concat_axis=0, tiled=True)]
    reduce_scatter x2 -> x0, waiting for transfers between devices: 71.9 us -> none  [the longest x1 38.4 us: per_device(): lax.psum_scatter(weight, 'ckpt', scatter_dimension=1, tiled=True)]
    all_to_all x2 -> x0, starting transfers between devices: 11.6 us -> none  [the longest x1 6.33 us: per_device(): lax.all_to_all(row_tags, 'vocab', split_axis=0, concat_axis=0, tiled=True)]
    dot_general x2 -> x0, matrix products: 10.2 us -> none  [the longest x1 5.11 us: per_device(): jnp.dot(selector, arrived.reshape(groups * capacity, width), preferred_el...]
    unnamed x4 -> x9, local copies, waits for them, and re-layouts: 0.01 us -> 5.38 us
    convert_element_type x3 -> x0, other arithmetic: 2.19 us -> none  [the longest x1 2.16 us: per_device(): return (numer / denom).astype(jnp.bfloat16)]
  transfers between devices with their start and end apart: 4 -> 0, of which waited for: 3 -> 0; matrix products, arithmetic and copies ran while one was open for 3% -> 0% of each run, Pallas kernels for 0% -> 0%
where the time goes in v1:
time: 112 us
  Pallas kernels  106 us (95%)
  local copies, waits for them, and re-layouts  6.15 us (5%)
    pallas_call x1, Pallas kernels, merge_rows(): pl.pallas_call(functools.partial(merge_kernel, groups, ckpts, CHUNKS), ou...  106 us
    unnamed x9, local copies, waits for them, and re-layouts  5.38 us

profile of v1, /device:TPU:0, one launch (start us, length us, event | category | flops | bytes accessed | tf_op | source)
XLA Modules:
  0.0 112.2 jit_solution(16657104140946937083)
XLA Ops:
  0.0 0.8 copy.5.ids_col_ref
  0.8 0.0 copy-start
  0.8 1.6 %copy-done = bf16[1,128,8192]{2,1,0:T(8,128)(2,1)S(1)} copy-done((bf16[1,128,8192]{2,1,0:T(8,128)(2,1)S(1)}, bf16[1,128,8192]{2,1,0:T(8,128)(2,1)}, u32[]{:S(2)}) %copy-start) | copy-done | bytes 2097176
  2.4 0.0 copy-start.1
  2.4 1.6 %copy-done.1 = bf16[1,128,8192]{2,1,0:T(8,128)(2,1)S(1)} copy-done((bf16[1,128,8192]{2,1,0:T(8,128)(2,1)S(1)}, bf16[1,128,8192]{2,1,0:T(8,128)(2,1)}, u32[]{:S(2)}) %copy-start.1) | copy-done | bytes 2097176
  3.9 0.0 copy-start.2
  3.9 0.8 copy-done.2
  4.7 0.0 copy-start.3
  4.7 0.7 copy-done.3
  5.4 106.0 %shard_map.46 = bf16[128,2048]{1,0:T(8,128)(2,1)S(1)} custom-call(s32[1,128]{1,0:T(1,128)S(1)} %bitcast.9, s32[128,1]{1,0:T(8,128)S(1)} %copy.5.ids_col_ref, bf16[128,8192]{1,0:T(8,128)(2,1)S(1)} %bitcast.5, f32[64,128]{1,0:T(8,128)S(1)} %bitcast.7, bf16[128,8192]{1,0:T(8,128)(2,1)S(1)} %bitcast.6), custom_call_target="tpu_custom_call" | custom-call | flops 1073741824 | bytes 5242880 | tf_op jit(solution)/shard_map/pallas_call | solution.py:237
  111.4 0.8 copy.7
Async XLA Ops:
  0.8 1.6 %copy-start = (bf16[1,128,8192]{2,1,0:T(8,128)(2,1)S(1)}, bf16[1,128,8192]{2,1,0:T(8,128)(2,1)}, u32[]{:S(2)}) copy-start(bf16[1,128,8192]{2,1,0:T(8,128)(2,1)} %param.5) | copy-start | bytes 6291460
  2.4 1.6 %copy-start.1 = (bf16[1,128,8192]{2,1,0:T(8,128)(2,1)S(1)}, bf16[1,128,8192]{2,1,0:T(8,128)(2,1)}, u32[]{:S(2)}) copy-start(bf16[1,128,8192]{2,1,0:T(8,128)(2,1)} %param.7) | copy-start | bytes 6291460
  3.9 0.8 copy-start.2
  4.7 0.7 copy-start.3

commit v2 on v1

--- a/solution.py
+++ b/solution.py
@@ -8,7 +8,7 @@
 from jax.sharding import PartitionSpec as P
 
 BLK = 128
-CHUNKS = 8
+CHUNKS = 16
 MESH = pl.DeviceIdType.MESH
 
 
@@ -19,14 +19,14 @@
     groups,
     ckpts,
     chunks,
-    ids_row_ref,
-    ids_col_ref,
+    ids_ref,
     grads_ref,
-    scales_ref,
+    all_scales_ref,
     tables_ref,
     out_ref,
     grads,
     tables,
+    scales_ref,
     match_ref,
     select_ref,
     tag_send,
@@ -68,11 +68,13 @@
 
     load_grads = pltpu.make_async_copy(grads_ref, grads, load_sem.at[0])
     load_tables = pltpu.make_async_copy(tables_ref, tables, load_sem.at[1])
+    load_scales = pltpu.make_async_copy(all_scales_ref, scales_ref, load_sem.at[2])
     load_grads.start()
+    load_scales.start()
     load_tables.start()
 
-    ids_row = ids_row_ref[...]
-    ids_col = ids_col_ref[...]
+    ids_row = ids_ref[...]
+    ids_col = jnp.broadcast_to(ids_row, (count, count)).T
     near_row = lax.rem(ids_row // rows - v + groups, groups)
     near_col = lax.rem(ids_col // rows - v + groups, groups)
     same = near_row == near_col
@@ -87,8 +89,8 @@
     ).astype(jnp.bfloat16)
     tags = jnp.sum(
         jnp.where(
-            lax.broadcasted_iota(jnp.int32, (count, slots), 1) == slot_col,
-            lax.rem(ids_col, rows),
+            lax.broadcasted_iota(jnp.int32, (count, slots), 1) == slot_col[:, 0:1],
+            lax.rem(ids_col[:, 0:1], rows),
             0,
         ),
         axis=0,
@@ -128,12 +130,7 @@
 
     order = sorted(range(1, groups), key=lambda j: -min(j, groups - j))
 
-    load_grads.wait()
-    pl.semaphore_wait(barrier, groups + ckpts - 2)
-    for j in order:
-        tag_copy(j).start()
-
-    def place(k, carry):
+    def place(k):
         block_scales = jnp.concatenate(
             [
                 scales_ref[pl.ds(q * (quarter // BLK) + k * blocks, blocks), :]
@@ -157,11 +154,25 @@
         recv[k, 0] = placed[0]
         for j in range(1, groups):
             send[k, j] = placed[j]
+
+    def start_rows(k):
         for j in order:
             row_copy(k, j).start()
+
+    load_grads.wait()
+    load_scales.wait()
+    place(0)
+    pl.semaphore_wait(barrier, groups + ckpts - 2)
+    for j in order:
+        tag_copy(j).start()
+    start_rows(0)
+
+    def place_next(k, carry):
+        place(k)
+        start_rows(k)
         return carry
 
-    lax.fori_loop(0, chunks, place, 0)
+    lax.fori_loop(1, chunks, place_next, 0)
 
     lane = lax.broadcasted_iota(jnp.int32, (1, slots), 1) // capacity
     arrived_tags = jnp.where(lane == 0, tags, 0)
@@ -237,11 +248,12 @@
     return pl.pallas_call(
         functools.partial(merge_kernel, groups, ckpts, CHUNKS),
         out_shape=jax.ShapeDtypeStruct((rows, width // ckpts), bf16),
-        in_specs=[vmem, vmem, hbm, vmem, hbm],
+        in_specs=[vmem, hbm, hbm, hbm],
         out_specs=vmem,
         scratch_shapes=[
             pltpu.VMEM((count, width), bf16),
             pltpu.VMEM((rows, width), bf16),
+            pltpu.VMEM((width // BLK, count), jnp.float32),
             pltpu.VMEM((slots, count), bf16),
             pltpu.VMEM((rows, slots), bf16),
             pltpu.VMEM((8, slots), jnp.int32),
@@ -250,7 +262,7 @@
             pltpu.VMEM((CHUNKS, groups, capacity, chunk_width), bf16),
             pltpu.VMEM((CHUNKS, ckpts, 2, rows, chunk_width // ckpts), bf16),
             pltpu.VMEM((CHUNKS, ckpts, 2, rows, chunk_width // ckpts), bf16),
-            dma((2,)),
+            dma((3,)),
             dma((groups,)),
             dma((groups,)),
             dma((CHUNKS, groups)),
@@ -259,7 +271,7 @@
             dma((CHUNKS, ckpts)),
         ],
         compiler_params=pltpu.CompilerParams(
-            collective_id=0, has_side_effects=True, vmem_limit_bytes=48 * 1024 * 1024
+            collective_id=0, has_side_effects=True, vmem_limit_bytes=60 * 1024 * 1024
         ),
         cost_estimate=pl.CostEstimate(
             flops=4 * slots * count * width,
@@ -268,7 +280,6 @@
         ),
     )(
         token_ids.reshape(1, count),
-        token_ids.reshape(count, 1),
         grad_values[0],
         grad_scales[0],
         tables[0],

time: 112 us -> 110 us (0.982)
  local copies, waits for them, and re-layouts: 6.15 us -> 1.88 us
  Pallas kernels: 106 us -> 108 us
    unnamed x9 -> x1, local copies, waits for them, and re-layouts: 5.38 us -> 1.88 us
    pallas_call x1, Pallas kernels: 106 us -> 108 us  [merge_rows(): pl.pallas_call(functools.partial(merge_kernel, groups, ckpts, CHUNKS), ou...]
where the time goes in v2:
time: 110 us
  Pallas kernels  108 us (98%)
  local copies, waits for them, and re-layouts  1.88 us (2%)
    pallas_call x1, Pallas kernels, merge_rows(): pl.pallas_call(functools.partial(merge_kernel, groups, ckpts, CHUNKS), ou...  108 us

profile of v2, /device:TPU:0, one launch (start us, length us, event | category | flops | bytes accessed | tf_op | source)
XLA Modules:
  0.0 110.3 jit_solution(5067951954005235333)
XLA Ops:
  0.0 108.4 %shard_map.46 = bf16[128,2048]{1,0:T(8,128)(2,1)} custom-call(s32[1,128]{1,0:T(1,128)} %bitcast.7, bf16[128,8192]{1,0:T(8,128)(2,1)} %bitcast.4, f32[64,128]{1,0:T(8,128)} %bitcast.6, bf16[128,8192]{1,0:T(8,128)(2,1)} %bitcast.5), custom_call_target="tpu_custom_call" | custom-call | flops 1073741824 | bytes 5242880 | tf_op jit(solution)/shard_map/pallas_call | solution.py:248
  108.4 1.9 %copy.6 = bf16[128,2048]{1,0:T(8,128)(2,1)} copy(bf16[128,2048]{1,0:T(8,128)(2,1)} %shard_map.46) | data formatting | bytes 1048576
